TPU v7x, 32 devices: a whole 2x2x4 slice. The times are simulated.
32 devices in a mesh: ha: 8 (over y, x, core), wa: 4 (over z).
Axes of the slice: x: 2, y: 2, z: 4, core: 2. Of those that a mesh axis runs over, the one named last changes fastest.
Arguments:
- tokens: bfloat16 [128, 64, 256], P('ha', 'wa'), may hold values from -6 to 6
- gain_attn: float32 [256], replicated, may hold values from 0.25 to 1.75
- qkv_fine: bfloat16 [256, 768], replicated, may hold values from -0.375 to 0.375
- scale_fine: float32 [4], replicated, may hold values from 2 to 24
- out_fine: bfloat16 [256, 256], replicated, may hold values from -0.375 to 0.375
- gain_ffn: float32 [256], replicated, may hold values from 0.25 to 1.75
- ffn_in: bfloat16 [256, 1536], replicated, may hold values from -0.375 to 0.375
- ffn_out: bfloat16 [768, 256], replicated, may hold values from -0.21875 to 0.21875
- up_proj: bfloat16 [256, 1024], replicated, may hold values from -0.375 to 0.375
- gain_coarse: float32 [1024], replicated, may hold values from 0.25 to 1.75
- qkv_coarse: bfloat16 [1024, 3072], replicated, may hold values from -0.1875 to 0.1875
- scale_coarse: float32 [16], replicated, may hold values from 2 to 24
- out_coarse: bfloat16 [1024, 1024], replicated, may hold values from -0.1875 to 0.1875
Outputs:
- fine_out: bfloat16 [128, 64, 256], P('ha', 'wa')
- coarse_out: bfloat16 [8, 4, 1024], P('ha', 'wa')
All inputs are finite; a program needn't handle non-finite values.
Results may differ from a plain program's by a relative error of at most 0.03.
Values may be sent and summed in bfloat16 or wider, within the bound.
No kernel may reach another device: no remote copies, remote signals or barrier semaphores. Data moves between devices by JAX's collectives and lax.ppermute only.
A program may use at most 128 MiB of HBM per device.

v0:
```python
import functools

import jax
import jax.numpy as jnp
from jax import lax
from jax.experimental import pallas as pl
from jax.experimental.pallas import tpu as pltpu
from jax.sharding import PartitionSpec as P

HD = 64
RADIUS = 3
LOG2E = 1.4426950408889634
BIG = 2.0**30
GELU = 0.7978845608028654
BF = jnp.bfloat16
F32 = jnp.float32
MIB = 1 << 20


def rounded_up(value, step):
    return -(-value // step) * step


def over(values, size):
    assert size & (size - 1) == 0
    return values >> (size.bit_length() - 1)


def dot(a, b):
    return jnp.dot(a, b, preferred_element_type=F32)


def dot_nt(a, b):
    return lax.dot_general(a, b, (((1,), (1,)), ((), ())), preferred_element_type=F32)


def dot_split(values, ones):
    high = values.astype(BF)
    low = (values - high.astype(F32)).astype(BF)
    return dot(high, ones) + dot(low, ones)


def same_head(size):
    left = over(lax.broadcasted_iota(jnp.int32, (size, 1), 0), HD)
    right = over(lax.broadcasted_iota(jnp.int32, (1, size), 1), HD)
    return jnp.where(left == right, 1.0, 0.0).astype(BF)


def head_norm(values, ones):
    return values * lax.rsqrt(dot((values * values).astype(BF), ones) * (1.0 / HD) + 1e-06)


def rms_factor(values):
    return lax.rsqrt(jnp.mean(values * values, -1, keepdims=True) + 1e-06)


def rms_norm(values, gain):
    return values * rms_factor(values) * gain


def head_factor(squares, factor):
    return factor * lax.rsqrt(squares * (factor * factor * (1.0 / HD)) + 1e-06)


def copies_of(pairs, sems):
    return [pltpu.make_async_copy(src, dst, sems.at[i]) for i, (src, dst) in enumerate(pairs)]


def start_all(copies):
    for copy in copies:
        copy.start()


def wait_all(copies):
    for copy in copies:
        copy.wait()


def after_starts(axis):
    return pl.when(lax.axis_index(axis) >= 0)


def strip_kernel(rows, cols, axis, tok_hbm, across_ref, within_ref, sems):
    count, strip = rows * cols, RADIUS * cols
    odd = lax.axis_index(axis) & 1
    last = count - strip
    first = pl.multiple_of(odd * last, 16)
    second = pl.multiple_of((1 - odd) * last, 16)
    copies = copies_of(
        [
            (tok_hbm.at[pl.ds(first, strip), :], across_ref),
            (tok_hbm.at[pl.ds(second, strip), :], within_ref),
        ],
        sems,
    )
    start_all(copies)
    wait_all(copies)


def edge_kernel(rows, cols, axes, tok_ref, across_ref, within_ref, after_ref, across_out, within_out):
    height = rows + 2 * RADIUS
    strip = RADIUS * cols
    padded = across_out.shape[0]
    odd, odd_col = lax.axis_index(axes[0]) & 1, lax.axis_index(axes[1]) & 1
    block = jnp.concatenate([tok_ref[...], across_ref[...], within_ref[...]], 0)
    out = lax.broadcasted_iota(jnp.int32, (padded, 1), 0)
    src = lax.broadcasted_iota(jnp.int32, (padded, block.shape[0]), 1)
    row = ((out * 21846) >> 16) - RADIUS
    col = out - 3 * (row + RADIUS)
    above = rows * cols + strip * odd + RADIUS * cols
    below = rows * cols + strip * (1 - odd) - rows * cols
    first = row * cols + col + jnp.where(row < 0, above, jnp.where(row >= rows, below, 0))
    first = jnp.where(out < height * RADIUS, first, -2 * cols)
    far = cols - RADIUS
    pick = jnp.where(src == first + far * odd_col, 1.0, 0.0).astype(BF)
    across_out[...] = dot(pick, block).astype(BF)
    pick = jnp.where(src == first + far * (1 - odd_col), 1.0, 0.0).astype(BF)
    within_out[...] = dot(pick, block).astype(BF)


def merge_kernel(
    after_ref, up_ref, gain_ref, scale_ref, head_ref, qkv_hbm,
    merged_ref, scale_out, weight_ref, scaled_ref, total_ref, sems,
):
    size = head_ref.shape[0]
    blocks = sems.shape[0]

    def span_of(block):
        return pl.ds(pl.multiple_of(block * size, size), size)

    def copy(block):
        return pltpu.make_async_copy(
            qkv_hbm.at[span_of(block + 1), :], weight_ref.at[span_of(block), :], sems.at[block]
        )

    for block in range(blocks):
        copy(block).start()
    lane = over(lax.broadcasted_iota(jnp.int32, scale_out.shape, 1), HD)
    scales = jnp.zeros(scale_out.shape, F32)
    for head in range(scale_ref.shape[1]):
        scales = jnp.where(lane == head, scale_ref[0:1, head : head + 1], scales)
    scale_out[...] = scales * (1.0 / HD)
    scaled_ref[...] = (up_ref[...].astype(F32) * gain_ref[...]).astype(BF)
    wide = 4 * size
    rows = scaled_ref[:, :size]

    def begin(part, carry):
        span = pl.ds(pl.multiple_of(part * wide, wide), wide)
        total_ref[:, span] = dot(rows, head_ref[:, span])
        return carry

    lax.fori_loop(0, merged_ref.shape[1] // wide, begin, 0)

    def step(block, carry):
        copy(block).wait()
        rows = scaled_ref[:, span_of(block + 1)]
        depth = span_of(block)
        for at in range(0, merged_ref.shape[1], size):
            span = slice(at, at + size)
            total = total_ref[:, span] + dot(rows, weight_ref[depth, span])
            total_ref[:, span] = total
            merged_ref[:, span] = total.astype(BF)
        return carry

    lax.fori_loop(0, blocks, step, 0)


def half_lanes():
    return lax.broadcasted_iota(jnp.int32, (1, 2 * HD), 1) < HD


def mask_columns(rows, cols):
    place = lax.broadcasted_iota(jnp.int32, (1, 2 * HD), 1) & (HD - 1)
    return place, place < rows, (place >= rows) & (place < rows + cols)


def query_columns(rows, cols):
    place, is_row, is_col = mask_columns(rows, cols)
    spot = lax.broadcasted_iota(jnp.int32, (rows * cols, 1), 0)
    hot = (is_row & (over(spot, cols) == place)) | (is_col & ((spot & (cols - 1)) == place - rows))
    return jnp.where(hot, 1.0, 0.0).astype(BF)


def key_columns(rows, cols, krow, kcol):
    place, is_row, is_col = mask_columns(rows, cols)
    far_row = jnp.abs(krow - place) > RADIUS
    far_col = jnp.abs(kcol - (place - rows)) > RADIUS
    return jnp.where((is_row & far_row) | (is_col & far_col), -BIG, 0.0).astype(BF)


def halo_columns(rows, cols, side, axes):
    strip = RADIUS * cols
    row_axis, col_axis = axes
    place_row, place_col = lax.axis_index(row_axis), lax.axis_index(col_axis)
    row0, col0 = place_row * rows, place_col * cols
    grid_rows = lax.axis_size(row_axis) * rows
    grid_cols = lax.axis_size(col_axis) * cols
    odd, odd_col = place_row & 1, place_col & 1
    row_at = (odd * (rows + RADIUS) - RADIUS, (1 - odd) * (rows + RADIUS) - RADIUS)
    col_at = (odd_col * (cols + RADIUS) - RADIUS, (1 - odd_col) * (cols + RADIUS) - RADIUS)
    spot = lax.broadcasted_iota(jnp.int32, (2 * strip + 2 * side, 1), 0)
    past_first = spot - strip
    past_strips = past_first - strip
    past_third = past_strips - side
    strip_at = jnp.where(past_first >= 0, past_first, spot)
    side_at = jnp.where(past_third >= 0, past_third, past_strips)
    side_row = (side_at * 21846) >> 16
    in_strip = past_strips < 0
    krow = jnp.where(
        in_strip,
        over(strip_at, cols) + jnp.where(past_first >= 0, row_at[1], row_at[0]),
        side_row - RADIUS,
    )
    kcol = jnp.where(
        in_strip,
        strip_at & (cols - 1),
        side_at - 3 * side_row + jnp.where(past_third >= 0, col_at[1], col_at[0]),
    )
    real = in_strip | (side_at < (rows + 2 * RADIUS) * RADIUS)
    real = real & (krow + row0 >= 0) & (krow + row0 < grid_rows)
    real = real & (kcol + col0 >= 0) & (kcol + col0 < grid_cols)
    return key_columns(rows, cols, jnp.where(real, krow, -1000), kcol)


def half_of(head):
    low = half_lanes()
    lanes = 2 * HD
    return (low if head % 2 == 0 else ~low), slice(head // 2 * lanes, (head // 2 + 1) * lanes)


def attend(head, query, key, value, key_mask, factor):
    mine, span = half_of(head)
    k = jnp.where(mine, key[:, span], key_mask)
    v = jnp.where(mine, value[:, span], jnp.ones((1, 2 * HD), BF))
    weights = jnp.exp2(dot_nt(query, k) * (factor * (LOG2E / HD))).astype(BF)
    return dot(weights, v)


def own_kernel(rows, cols, heads, side, axes, *refs):
    count = (len(refs) - 7) // 2
    ins, qkv_c_hbm, outs = refs[:count], refs[count], refs[count + 1 : 2 * count + 1]
    head_ref, query_ref, acc_ref, ones_ref, mask_ref, sems = refs[2 * count + 1 :]
    tok_ref, qkv_ref, gain_ref, scale_ref = outs[:4]
    head = (qkv_c_hbm.at[pl.ds(0, head_ref.shape[0]), :], head_ref)
    copies = copies_of(list(zip(ins, outs)) + [head], sems)
    start_all(copies)

    @after_starts(axes[0])
    def _():
        width = heads * HD
        ones = same_head(width)
        ones_ref[...] = ones
        mask_ref[...] = halo_columns(rows, cols, side, axes)
        query_mask = query_columns(rows, cols)
        spot = lax.broadcasted_iota(jnp.int32, (rows * cols, 1), 0)
        key_mask = key_columns(rows, cols, over(spot, cols), spot & (cols - 1))
        wait_all(copies[:4])
        normed = rms_norm(tok_ref[...].astype(F32), gain_ref[...]).astype(BF)
        query = head_norm(dot(normed, qkv_ref[:, :width]), ones).astype(BF)
        key = head_norm(dot(normed, qkv_ref[:, width : 2 * width]), ones).astype(BF)
        value = dot(normed, qkv_ref[:, 2 * width :]).astype(BF)
        for head in range(heads):
            factor = scale_ref[0:1, head : head + 1]
            mine, span = half_of(head)
            masked = jnp.where(mine, query[:, span], query_mask)
            query_ref[head] = masked
            acc_ref[head] = attend(head, masked, key, value, key_mask, factor)

    wait_all(copies[4:])


def fine_kernel(
    heads, axis,
    tok_ref, halo_refs, query_ref, acc_ref, ones_ref, mask_ref, gain_attn_ref, qkv_ref, scale_ref,
    out_ref, gain_ffn_ref, ffn_in_ref, ffn_out_ref, after_ref, out_c_hbm,
    fine_ref, pooled_ref, out_c_ref, sems,
):
    copies = copies_of([(out_c_hbm, out_c_ref)], sems)
    start_all(copies)

    @after_starts(axis)
    def _():
        width = heads * HD
        halo = jnp.concatenate([ref[...] for ref in halo_refs], 0)
        halo = halo.astype(F32)
        scaled = (halo * gain_attn_ref[...]).astype(BF)
        halo_rms = rms_factor(halo)
        ones = ones_ref[...]
        key = dot(scaled, qkv_ref[:, width : 2 * width])
        key = (key * head_factor(dot((key * key).astype(BF), ones), halo_rms)).astype(BF)
        value = (dot(scaled, qkv_ref[:, 2 * width :]) * halo_rms).astype(BF)

        key_mask = mask_ref[...]
        low = half_lanes()
        parts = []
        for pair in range(heads // 2):
            sums = []
            for head in (2 * pair, 2 * pair + 1):
                factor = scale_ref[0:1, head : head + 1]
                sums.append(acc_ref[head] + attend(head, query_ref[head], key, value, key_mask, factor))
            top = jnp.where(low, sums[0], sums[1])
            bottom = pltpu.roll(jnp.where(low, sums[1], sums[0]), HD, 1)
            parts.append((top / bottom).astype(BF))
        attn = jnp.concatenate(parts, 1)

        h1 = (tok_ref[...].astype(F32) + dot(attn, out_ref[...])).astype(BF)
        h1_wide = h1.astype(F32)
        scaled = (h1_wide * gain_ffn_ref[...]).astype(BF)
        h1_rms = rms_factor(h1_wide)
        hidden = ffn_out_ref.shape[0]
        gate = dot(scaled, ffn_in_ref[:, :hidden]) * h1_rms
        up = dot(scaled, ffn_in_ref[:, hidden:]) * (0.5 * h1_rms)
        inner = gate * (GELU + (GELU * 0.044715) * (gate * gate))
        gated = (gate * up * (1.0 + jnp.tanh(inner))).astype(BF)
        fine = (h1_wide + dot(gated, ffn_out_ref[...])).astype(BF)
        fine_ref[...] = fine
        pooled = jnp.mean(fine.astype(F32), 0, keepdims=True).astype(BF).astype(F32)
        for part in range(pooled_ref.shape[1]):
            pooled_ref[:, part, :] = jnp.broadcast_to(
                pooled[:, part * 128 : (part + 1) * 128], (pooled_ref.shape[0], 128)
            )

    wait_all(copies)


def coarse_kernel(
    axes, pooled_ref, up_ref, merged_ref, scale_ref, out_ref, fine_ref, ones_ref,
    coarse_out_ref, fine_hbm,
    coarse_ref, sems,
):
    copies = copies_of([(fine_ref, fine_hbm)], sems)
    start_all(copies)
    width = out_ref.shape[0]
    row_axis, col_axis = axes
    mine = lax.axis_index(row_axis) * lax.axis_size(col_axis) + lax.axis_index(col_axis)
    pooled = jnp.concatenate([pooled_ref[:, part, :] for part in range(pooled_ref.shape[1])], 1).astype(BF)
    coarse = dot(pooled, up_ref[...]).astype(BF).astype(F32)
    coarse_ref[...] = coarse
    mine_row = [pooled_ref[pl.ds(mine, 1), part, :] for part in range(pooled_ref.shape[1])]
    query = dot(jnp.concatenate(mine_row, 1).astype(BF), merged_ref[:, :width])
    key = dot(pooled, merged_ref[:, width : 2 * width])
    value = dot(pooled, merged_ref[:, 2 * width :])
    own = coarse_ref[pl.ds(mine, 1), :]
    rms = rms_factor(coarse)
    group = 4 * HD
    spans = [slice(at, at + group) for at in range(0, width, group)]
    tall = jnp.concatenate([key[:, span] for span in spans], 0)
    queries = [query[:, span] for span in spans]
    cross = jnp.concatenate([key[:, span] * q for span, q in zip(spans, queries)], 0)
    ones = ones_ref[...]
    query_squares = jnp.concatenate([q * q for q in queries], 0).astype(BF)
    query_norm = head_factor(dot(query_squares, ones), rms_factor(own))
    key_norm = head_factor(dot((tall * tall).astype(BF), ones), jnp.concatenate([rms] * len(spans), 0))
    scores = dot_split(cross, ones) * key_norm
    count = key.shape[0]
    parts = []
    for at, span in enumerate(spans):
        factor = query_norm[at : at + 1] * scale_ref[:, span]
        expo = jnp.exp(scores[at * count : (at + 1) * count] * factor)
        total = jnp.sum(expo, 0, keepdims=True)
        parts.append(jnp.sum(expo * rms * value[:, span], 0, keepdims=True) / total)
    cattn = jnp.concatenate(parts, 1).astype(BF)
    coarse_out_ref[...] = (own + dot(cattn, out_ref[...])).astype(BF)
    wait_all(copies)


def vmem(count):
    return [pl.BlockSpec(memory_space=pltpu.VMEM)] * count


def anywhere(count):
    return [pl.BlockSpec(memory_space=pl.ANY)] * count


def in_vmem(arrays):
    return [pltpu.with_memory_space_constraint(array, pltpu.VMEM) for array in arrays]


def in_hbm(arrays):
    return [pltpu.with_memory_space_constraint(array, pltpu.HBM) for array in arrays]


def shards(
    tokens, gain_attn, qkv_fine, scale_fine, out_fine, gain_ffn, ffn_in, ffn_out,
    up_proj, gain_coarse, qkv_coarse, scale_coarse, out_coarse,
):
    rows, cols, width = tokens.shape
    count = rows * cols
    strip = RADIUS * cols
    side = rounded_up((rows + 2 * RADIUS) * RADIUS, 16)
    heads = width // HD
    width_c = out_coarse.shape[0]
    devices = lax.axis_size("ha") * lax.axis_size("wa")
    axes = ("ha", "wa")
    params = pltpu.CompilerParams(vmem_limit_bytes=16 * MIB)

    def swapped(array, axis, first):
        pairs = [(i, i + 1) for i in range(first, lax.axis_size(axis) - 1, 2)]
        return lax.ppermute(array, axis, pairs + [(j, i) for i, j in pairs])

    flat = tokens.reshape(count, width)
    across, within = pl.pallas_call(
        functools.partial(strip_kernel, rows, cols, "ha"),
        out_shape=[pltpu.VMEM((strip, width), BF)] * 2,
        in_specs=anywhere(1),
        out_specs=vmem(2),
        scratch_shapes=[pltpu.SemaphoreType.DMA((2,))],
        compiler_params=params,
        name="strips",
    )(*in_hbm([flat]))
    across = swapped(across, "ha", 1)
    within = swapped(within, "ha", 0)

    block = 256
    weights = [
        flat, qkv_fine, gain_attn.reshape(1, -1), scale_fine.reshape(1, -1),
        up_proj, gain_coarse.reshape(1, -1), scale_coarse.reshape(1, -1),
        out_fine, gain_ffn.reshape(1, -1), ffn_in, ffn_out,
    ]
    *weights, head, query, acc, ones, mask = pl.pallas_call(
        functools.partial(own_kernel, rows, cols, heads, side, axes),
        out_shape=[pltpu.VMEM(array.shape, array.dtype) for array in weights]
        + [
            pltpu.VMEM((block, 3 * width_c), BF),
            pltpu.VMEM((heads, count, 2 * HD), BF),
            pltpu.VMEM((heads, count, 2 * HD), F32),
            pltpu.VMEM((4 * HD, 4 * HD), BF),
            pltpu.VMEM((2 * strip + 2 * side, 2 * HD), BF),
        ],
        in_specs=anywhere(len(weights) + 1),
        out_specs=vmem(len(weights) + 5),
        scratch_shapes=[pltpu.SemaphoreType.DMA((len(weights) + 1,))],
        compiler_params=params,
        cost_estimate=pl.CostEstimate(
            flops=2 * count * width * (3 * width + 2 * count), bytes_accessed=4 * MIB, transcendentals=0
        ),
        name="own",
    )(*in_hbm(weights + [qkv_coarse]))
    tok_v, qkv_v, gain_attn_v, scale_v, up_v, gain_c_v, scale_c_v = weights[:7]
    out_v, gain_ffn_v, ffn_in_v, ffn_out_v = weights[7:]

    across_edge, within_edge = pl.pallas_call(
        functools.partial(edge_kernel, rows, cols, axes),
        out_shape=[pltpu.VMEM((side, width), BF)] * 2,
        in_specs=vmem(4),
        out_specs=vmem(2),
        compiler_params=params,
        name="edges",
    )(*in_vmem([tok_v, across, within, query]))
    across_side = swapped(across_edge, "wa", 1)
    within_side = swapped(within_edge, "wa", 0)

    merged, scale_lanes = pl.pallas_call(
        merge_kernel,
        out_shape=[pltpu.VMEM((width, 3 * width_c), BF), pltpu.VMEM((1, width_c), F32)],
        in_specs=vmem(5) + anywhere(1),
        out_specs=vmem(2),
        scratch_shapes=[
            pltpu.VMEM((width_c - block, 3 * width_c), BF),
            pltpu.VMEM(up_proj.shape, BF),
            pltpu.VMEM((width, 3 * width_c), F32),
            pltpu.SemaphoreType.DMA((width_c // block - 1,)),
        ],
        compiler_params=params,
        cost_estimate=pl.CostEstimate(
            flops=6 * width * width_c * width_c, bytes_accessed=8 * MIB, transcendentals=0
        ),
        name="merge",
    )(*in_vmem([within_edge, up_v, gain_c_v, scale_c_v, head]), *in_hbm([qkv_coarse]))

    def fine_body(tok_ref, *refs):
        fine_kernel(heads, axes[0], tok_ref, refs[:4], *refs[4:])

    fine, pooled, out_c_v = pl.pallas_call(
        fine_body,
        out_shape=[
            pltpu.VMEM((count, width), BF),
            pltpu.VMEM((devices, width // 128, 128), F32),
            pltpu.VMEM(out_coarse.shape, BF),
        ],
        in_specs=vmem(17) + anywhere(1),
        out_specs=vmem(3),
        scratch_shapes=[pltpu.SemaphoreType.DMA((1,))],
        compiler_params=params,
        name="fine",
    )(
        *in_vmem(
            [tok_v, across, within, across_side, within_side, query, acc, ones, mask, gain_attn_v, qkv_v, scale_v]
            + [out_v, gain_ffn_v, ffn_in_v, ffn_out_v, merged]
        ),
        *in_hbm([out_coarse]),
    )

    every = lax.all_to_all(pooled, axes, split_axis=0, concat_axis=0, tiled=True)
    coarse_out, fine = pl.pallas_call(
        functools.partial(coarse_kernel, axes),
        out_shape=[
            jax.ShapeDtypeStruct((1, width_c), BF),
            jax.ShapeDtypeStruct((count, width), BF),
        ],
        in_specs=vmem(7),
        out_specs=vmem(1) + anywhere(1),
        scratch_shapes=[pltpu.VMEM((devices, width_c), F32), pltpu.SemaphoreType.DMA((1,))],
        compiler_params=params,
        name="coarse",
    )(*in_vmem([every, up_v, merged, scale_lanes, out_c_v, fine, ones]))
    return fine.reshape(rows, cols, width), coarse_out.reshape(1, 1, width_c)


def solution(mesh):
    return jax.shard_map(
        shards,
        mesh=mesh,
        in_specs=(P("ha", "wa", None), P(), P(), P(), P(), P(), P(), P(), P(), P(), P(), P(), P()),
        out_specs=(P("ha", "wa", None), P("ha", "wa", None)),
        check_vma=False,
    )
```

profile of v0, /device:TPU:0, one launch (start us, length us, event | category | flops | bytes accessed | tf_op | source)
XLA Modules:
  0.0 30.8 jit_solution(883814596542441736)
XLA Ops:
  0.6 0.8 %strips.1 = (bf16[48,256]{1,0:T(8,128)(2,1)S(1)}, bf16[48,256]{1,0:T(8,128)(2,1)S(1)}) custom-call(bf16[256,256]{1,0:T(8,128)(2,1)} %bitcast.8), custom_call_target="tpu_custom_call" | custom-call | tf_op jit(solution)/shard_map/strips/pallas_call | solution.py:402
  1.4 0.7 %collective-permute-start = (bf16[48,256]{1,0:T(8,128)(2,1)S(1)}, bf16[48,256]{1,0:T(8,128)(2,1)S(1)}, u32[]{:S(2)}, u32[]{:S(2)}) collective-permute-start(bf16[48,256]{1,0:T(8,128)(2,1)S(1)} %get-tuple-element.30), channel_id=1, source_target_pairs={{4,8},{12,16},{20,24},{8,4},{16,12},{24,20},{5,9},{13,17},{21,25},... | collective-permute-start | bytes 73736 | tf_op jit(solution)/shard_map/ppermute | solution.py:399
  2.1 4.4 %collective-permute-start.1 = (bf16[48,256]{1,0:T(8,128)(2,1)S(1)}, bf16[48,256]{1,0:T(8,128)(2,1)S(1)}, u32[]{:S(2)}, u32[]{:S(2)}) collective-permute-start(bf16[48,256]{1,0:T(8,128)(2,1)S(1)} %get-tuple-element.31), channel_id=1, source_target_pairs={{0,4},{8,12},{16,20},{24,28},{4,0},{12,8},{20,16},{28,24},{1,5},{9... | collective-permute-start | bytes 73736 | tf_op jit(solution)/shard_map/ppermute | solution.py:399
  6.5 2.3 %own.1 = (bf16[256,256]{1,0:T(8,128)(2,1)S(1)}, bf16[256,768]{1,0:T(8,128)(2,1)S(1)}, f32[1,256]{1,0:T(1,128)S(1)}, f32[1,4]{1,0:T(1,128)S(1)}, bf16[256,1024]{1...) custom-call(bf16[256,256]{1,0:T(8,128)(2,1)} %bitcast.9, ...), custom_call_target="tpu_custom_call" | custom-call | flops 167772160 | bytes 4194304 | tf_op jit(solution)/shard_map/own/pallas_call | solution.py:420
  8.8 0.0 collective-permute-done.across_ref.refs_0_
  8.8 0.0 collective-permute-done.1.within_ref.refs_1_
  8.8 0.2 edges.1
  9.0 0.7 %collective-permute-start.2 = (bf16[80,256]{1,0:T(8,128)(2,1)S(1)}, bf16[80,256]{1,0:T(8,128)(2,1)S(1)}, u32[]{:S(2)}, u32[]{:S(2)}) collective-permute-start(bf16[80,256]{1,0:T(8,128)(2,1)S(1)} %get-tuple-element.33), channel_id=1, source_target_pairs={{1,2},{2,1},{5,6},{6,5},{9,10},{10,9},{13,14},{14,13},{17,18},{18,... | collective-permute-start | bytes 122888 | tf_op jit(solution)/shard_map/ppermute | solution.py:399
  9.7 4.5 %collective-permute-start.3 = (bf16[80,256]{1,0:T(8,128)(2,1)S(1)}, bf16[80,256]{1,0:T(8,128)(2,1)S(1)}, u32[]{:S(2)}, u32[]{:S(2)}) collective-permute-start(bf16[80,256]{1,0:T(8,128)(2,1)S(1)} %get-tuple-element.34.after_ref), channel_id=1, source_target_pairs={{0,1},{2,3},{1,0},{3,2},{4,5},{6,7},{5,4},{7,6},{8,9},{10,11},{9,8... | collective-permute-start | bytes 122888 | tf_op jit(solution)/shard_map/ppermute | solution.py:399
  14.1 3.2 %merge.1 = (bf16[256,3072]{1,0:T(8,128)(2,1)S(1)}, f32[1,1024]{1,0:T(1,128)S(1)}) custom-call(bf16[80,256]{1,0:T(8,128)(2,1)S(1)} %get-tuple-element.34.after_ref, bf16[256,1024]{1,0:T(8,128)(2,1)S(1)} %get-tuple-element.45.up_ref, f32[1,1024]{1,0:T(1,128)S(1)} %get-tuple-element.46.gain_ref, f32[1,16]{1,0:T(1,128)S(1)} %get-tuple-element.47.scale_ref, ...), custom_call_target="tpu_custom_call" | custom-call | flops 1610612736 | bytes 8388608 | tf_op jit(solution)/shard_map/merge/pallas_call | solution.py:453
  17.3 0.0 collective-permute-done.2.refs_2_
  17.3 0.0 collective-permute-done.3.refs_3_
  17.4 1.7 %fine.1 = (bf16[256,256]{1,0:T(8,128)(2,1)S(1)}, f32[32,2,128]{2,1,0:T(2,128)S(1)}, bf16[1024,1024]{1,0:T(8,128)(2,1)S(1)}) custom-call(bf16[256,256]{1,0:T(8,128)(2,1)S(1)} %get-tuple-element.29.tok_ref, bf16[48,256]{1,0:T(8,128)(2,1)S(1)} %collective-permute-done.across_ref.refs_0_, bf16[48,256]{1,0:T(8,128)(2,1)S(1)} %collective-permute-done.1.within_ref.refs_1_, ...), custom_call_target="tpu_custom_call" | custom-call | tf_op jit(solution)/shard_map/fine/pallas_call | solution.py:474
  19.1 10.1 %all_to_all.5.pooled_ref = f32[32,2,128]{2,1,0:T(2,128)S(1)} all-to-all(f32[32,2,128]{2,1,0:T(2,128)S(1)} %get-tuple-element.50), channel_id=1, replica_groups=mesh['ha'=8,'wa'=4] {'ha','wa'}, dimensions={0} | all-to-all | bytes 65536 | tf_op jit(solution)/shard_map/all_to_all | solution.py:494
  29.2 1.5 %coarse.1 = (bf16[1,1024]{1,0:T(2,128)(2,1)}, bf16[256,256]{1,0:T(8,128)(2,1)}) custom-call(f32[32,2,128]{2,1,0:T(2,128)S(1)} %all_to_all.5.pooled_ref, bf16[256,1024]{1,0:T(8,128)(2,1)S(1)} %get-tuple-element.45.up_ref, bf16[256,3072]{1,0:T(8,128)(2,1)S(1)} %get-tuple-element.49.refs_15_.merged_ref, f32[1,1024]{1,0:T(1,128)S(1)} %get-tuple-element.51.scale_ref, ...), custom_call_target="tpu_custom_call" | custom-call | tf_op jit(solution)/shard_map/coarse/pallas_call | solution.py:495
Async XLA Ops:
  1.4 7.4 %collective-permute-start = (bf16[48,256]{1,0:T(8,128)(2,1)S(1)}, bf16[48,256]{1,0:T(8,128)(2,1)S(1)}, u32[]{:S(2)}, u32[]{:S(2)}) collective-permute-start(bf16[48,256]{1,0:T(8,128)(2,1)S(1)} %get-tuple-element.30), channel_id=1, source_target_pairs={{4,8},{12,16},{20,24},{8,4},{16,12},{24,20},{5,9},{13,17},{21,25},... | collective-permute-start | bytes 73736 | tf_op jit(solution)/shard_map/ppermute | solution.py:399
  2.1 6.7 %collective-permute-start.1 = (bf16[48,256]{1,0:T(8,128)(2,1)S(1)}, bf16[48,256]{1,0:T(8,128)(2,1)S(1)}, u32[]{:S(2)}, u32[]{:S(2)}) collective-permute-start(bf16[48,256]{1,0:T(8,128)(2,1)S(1)} %get-tuple-element.31), channel_id=1, source_target_pairs={{0,4},{8,12},{16,20},{24,28},{4,0},{12,8},{20,16},{28,24},{1,5},{9... | collective-permute-start | bytes 73736 | tf_op jit(solution)/shard_map/ppermute | solution.py:399
  9.0 8.3 %collective-permute-start.2 = (bf16[80,256]{1,0:T(8,128)(2,1)S(1)}, bf16[80,256]{1,0:T(8,128)(2,1)S(1)}, u32[]{:S(2)}, u32[]{:S(2)}) collective-permute-start(bf16[80,256]{1,0:T(8,128)(2,1)S(1)} %get-tuple-element.33), channel_id=1, source_target_pairs={{1,2},{2,1},{5,6},{6,5},{9,10},{10,9},{13,14},{14,13},{17,18},{18,... | collective-permute-start | bytes 122888 | tf_op jit(solution)/shard_map/ppermute | solution.py:399
  9.7 7.7 %collective-permute-start.3 = (bf16[80,256]{1,0:T(8,128)(2,1)S(1)}, bf16[80,256]{1,0:T(8,128)(2,1)S(1)}, u32[]{:S(2)}, u32[]{:S(2)}) collective-permute-start(bf16[80,256]{1,0:T(8,128)(2,1)S(1)} %get-tuple-element.34.after_ref), channel_id=1, source_target_pairs={{0,1},{2,3},{1,0},{3,2},{4,5},{6,7},{5,4},{7,6},{8,9},{10,11},{9,8... | collective-permute-start | bytes 122888 | tf_op jit(solution)/shard_map/ppermute | solution.py:399
where the time goes:
time: 31 us; the launch traced here: 30.8 us
  starting transfers between devices  10.2 us (33%)
  blocking collectives  10.1 us (33%)
  Pallas kernels  9.76 us (31%)
  between operations  0.71 us (2%)
    ppermute x4, starting transfers between devices, swapped(): return lax.ppermute(array, axis, pairs + [(j, i) for i, j in pairs])  10.2 us
    all_to_all x1, blocking collectives, shards(): lax.all_to_all(pooled, axes, split_axis=0, concat_axis=0, tiled=True)  10.1 us
    pallas_call x1, Pallas kernels, shards(): pl.pallas_call(merge_kernel, out_shape=[pltpu.VMEM((width, 3 * width_c),...  3.18 us
    pallas_call x1, Pallas kernels, shards(): pl.pallas_call(functools.partial(own_kernel, rows, cols, heads, side, axe...  2.33 us
    pallas_call x1, Pallas kernels, shards(): pl.pallas_call(fine_body, out_shape=[pltpu.VMEM((count, width), BF), pltp...  1.74 us
    pallas_call x1, Pallas kernels, shards(): pl.pallas_call(functools.partial(coarse_kernel, axes), out_shape=[jax.Sha...  1.53 us
    pallas_call x1, Pallas kernels, shards(): pl.pallas_call(functools.partial(strip_kernel, rows, cols, 'ha'), out_sha...  0.79 us
  transfers between devices with their start and end apart: 4, of which 0 were waited for; matrix products, arithmetic and copies ran while one was open for 0% of the time, Pallas kernels for 18%

commit v1 on v0

--- a/solution.py
+++ b/solution.py
@@ -348,11 +348,13 @@
     queries = [query[:, span] for span in spans]
     cross = jnp.concatenate([key[:, span] * q for span, q in zip(spans, queries)], 0)
     ones = ones_ref[...]
-    query_squares = jnp.concatenate([q * q for q in queries], 0).astype(BF)
-    query_norm = head_factor(dot(query_squares, ones), rms_factor(own))
-    key_norm = head_factor(dot((tall * tall).astype(BF), ones), jnp.concatenate([rms] * len(spans), 0))
-    scores = dot_split(cross, ones) * key_norm
+    squares = jnp.concatenate([q * q for q in queries], 0)
+    sums = dot(jnp.concatenate([tall * tall, cross, squares], 0).astype(BF), ones)
     count = key.shape[0]
+    total = count * len(spans)
+    key_norm = head_factor(sums[:total], jnp.concatenate([rms] * len(spans), 0))
+    scores = sums[total : 2 * total] * key_norm
+    query_norm = head_factor(sums[2 * total :], rms_factor(own))
     parts = []
     for at, span in enumerate(spans):
         factor = query_norm[at : at + 1] * scale_ref[:, span]

time: 31 us -> 31 us (level)
  no operation moved by 1% of the time
where the time goes in v1:
time: 31 us; the launch traced here: 30.8 us
  starting transfers between devices  10.2 us (33%)
  blocking collectives  10.1 us (33%)
  Pallas kernels  9.79 us (32%)
  between operations  0.71 us (2%)
    ppermute x4, starting transfers between devices, swapped(): return lax.ppermute(array, axis, pairs + [(j, i) for i, j in pairs])  10.2 us
    all_to_all x1, blocking collectives, shards(): lax.all_to_all(pooled, axes, split_axis=0, concat_axis=0, tiled=True)  10.1 us
    pallas_call x1, Pallas kernels, shards(): pl.pallas_call(merge_kernel, out_shape=[pltpu.VMEM((width, 3 * width_c),...  3.18 us
    pallas_call x1, Pallas kernels, shards(): pl.pallas_call(functools.partial(own_kernel, rows, cols, heads, side, axe...  2.33 us
    pallas_call x1, Pallas kernels, shards(): pl.pallas_call(fine_body, out_shape=[pltpu.VMEM((count, width), BF), pltp...  1.74 us
    pallas_call x1, Pallas kernels, shards(): pl.pallas_call(functools.partial(coarse_kernel, axes), out_shape=[jax.Sha...  1.56 us
    pallas_call x1, Pallas kernels, shards(): pl.pallas_call(functools.partial(strip_kernel, rows, cols, 'ha'), out_sha...  0.79 us
  transfers between devices with their start and end apart: 4, of which 0 were waited for; matrix products, arithmetic and copies ran while one was open for 0% of the time, Pallas kernels for 18%

profile of v1, /device:TPU:0, one launch (start us, length us, event | category | flops | bytes accessed | tf_op | source)
XLA Modules:
  0.0 30.8 jit_solution(6050977387742139756)
XLA Ops:
  0.6 0.8 %strips.1 = (bf16[48,256]{1,0:T(8,128)(2,1)S(1)}, bf16[48,256]{1,0:T(8,128)(2,1)S(1)}) custom-call(bf16[256,256]{1,0:T(8,128)(2,1)} %bitcast.8), custom_call_target="tpu_custom_call" | custom-call | tf_op jit(solution)/shard_map/strips/pallas_call | solution.py:404
  1.4 0.7 %collective-permute-start = (bf16[48,256]{1,0:T(8,128)(2,1)S(1)}, bf16[48,256]{1,0:T(8,128)(2,1)S(1)}, u32[]{:S(2)}, u32[]{:S(2)}) collective-permute-start(bf16[48,256]{1,0:T(8,128)(2,1)S(1)} %get-tuple-element.30), channel_id=1, source_target_pairs={{4,8},{12,16},{20,24},{8,4},{16,12},{24,20},{5,9},{13,17},{21,25},... | collective-permute-start | bytes 73736 | tf_op jit(solution)/shard_map/ppermute | solution.py:401
  2.1 4.4 %collective-permute-start.1 = (bf16[48,256]{1,0:T(8,128)(2,1)S(1)}, bf16[48,256]{1,0:T(8,128)(2,1)S(1)}, u32[]{:S(2)}, u32[]{:S(2)}) collective-permute-start(bf16[48,256]{1,0:T(8,128)(2,1)S(1)} %get-tuple-element.31), channel_id=1, source_target_pairs={{0,4},{8,12},{16,20},{24,28},{4,0},{12,8},{20,16},{28,24},{1,5},{9... | collective-permute-start | bytes 73736 | tf_op jit(solution)/shard_map/ppermute | solution.py:401
  6.5 2.3 %own.1 = (bf16[256,256]{1,0:T(8,128)(2,1)S(1)}, bf16[256,768]{1,0:T(8,128)(2,1)S(1)}, f32[1,256]{1,0:T(1,128)S(1)}, f32[1,4]{1,0:T(1,128)S(1)}, bf16[256,1024]{1...) custom-call(bf16[256,256]{1,0:T(8,128)(2,1)} %bitcast.9, ...), custom_call_target="tpu_custom_call" | custom-call | flops 167772160 | bytes 4194304 | tf_op jit(solution)/shard_map/own/pallas_call | solution.py:422
  8.8 0.0 collective-permute-done.across_ref.refs_0_
  8.8 0.0 collective-permute-done.1.within_ref.refs_1_
  8.8 0.2 edges.1
  9.0 0.7 %collective-permute-start.2 = (bf16[80,256]{1,0:T(8,128)(2,1)S(1)}, bf16[80,256]{1,0:T(8,128)(2,1)S(1)}, u32[]{:S(2)}, u32[]{:S(2)}) collective-permute-start(bf16[80,256]{1,0:T(8,128)(2,1)S(1)} %get-tuple-element.33), channel_id=1, source_target_pairs={{1,2},{2,1},{5,6},{6,5},{9,10},{10,9},{13,14},{14,13},{17,18},{18,... | collective-permute-start | bytes 122888 | tf_op jit(solution)/shard_map/ppermute | solution.py:401
  9.7 4.5 %collective-permute-start.3 = (bf16[80,256]{1,0:T(8,128)(2,1)S(1)}, bf16[80,256]{1,0:T(8,128)(2,1)S(1)}, u32[]{:S(2)}, u32[]{:S(2)}) collective-permute-start(bf16[80,256]{1,0:T(8,128)(2,1)S(1)} %get-tuple-element.34.after_ref), channel_id=1, source_target_pairs={{0,1},{2,3},{1,0},{3,2},{4,5},{6,7},{5,4},{7,6},{8,9},{10,11},{9,8... | collective-permute-start | bytes 122888 | tf_op jit(solution)/shard_map/ppermute | solution.py:401
  14.1 3.2 %merge.1 = (bf16[256,3072]{1,0:T(8,128)(2,1)S(1)}, f32[1,1024]{1,0:T(1,128)S(1)}) custom-call(bf16[80,256]{1,0:T(8,128)(2,1)S(1)} %get-tuple-element.34.after_ref, bf16[256,1024]{1,0:T(8,128)(2,1)S(1)} %get-tuple-element.45.up_ref, f32[1,1024]{1,0:T(1,128)S(1)} %get-tuple-element.46.gain_ref, f32[1,16]{1,0:T(1,128)S(1)} %get-tuple-element.47.scale_ref, ...), custom_call_target="tpu_custom_call" | custom-call | flops 1610612736 | bytes 8388608 | tf_op jit(solution)/shard_map/merge/pallas_call | solution.py:455
  17.3 0.0 collective-permute-done.2.refs_2_
  17.3 0.0 collective-permute-done.3.refs_3_
  17.4 1.7 %fine.1 = (bf16[256,256]{1,0:T(8,128)(2,1)S(1)}, f32[32,2,128]{2,1,0:T(2,128)S(1)}, bf16[1024,1024]{1,0:T(8,128)(2,1)S(1)}) custom-call(bf16[256,256]{1,0:T(8,128)(2,1)S(1)} %get-tuple-element.29.tok_ref, bf16[48,256]{1,0:T(8,128)(2,1)S(1)} %collective-permute-done.across_ref.refs_0_, bf16[48,256]{1,0:T(8,128)(2,1)S(1)} %collective-permute-done.1.within_ref.refs_1_, ...), custom_call_target="tpu_custom_call" | custom-call | tf_op jit(solution)/shard_map/fine/pallas_call | solution.py:476
  19.1 10.1 %all_to_all.5.pooled_ref = f32[32,2,128]{2,1,0:T(2,128)S(1)} all-to-all(f32[32,2,128]{2,1,0:T(2,128)S(1)} %get-tuple-element.50), channel_id=1, replica_groups=mesh['ha'=8,'wa'=4] {'ha','wa'}, dimensions={0} | all-to-all | bytes 65536 | tf_op jit(solution)/shard_map/all_to_all | solution.py:496
  29.2 1.6 %coarse.1 = (bf16[1,1024]{1,0:T(2,128)(2,1)}, bf16[256,256]{1,0:T(8,128)(2,1)}) custom-call(f32[32,2,128]{2,1,0:T(2,128)S(1)} %all_to_all.5.pooled_ref, bf16[256,1024]{1,0:T(8,128)(2,1)S(1)} %get-tuple-element.45.up_ref, bf16[256,3072]{1,0:T(8,128)(2,1)S(1)} %get-tuple-element.49.refs_15_.merged_ref, f32[1,1024]{1,0:T(1,128)S(1)} %get-tuple-element.51.scale_ref, ...), custom_call_target="tpu_custom_call" | custom-call | tf_op jit(solution)/shard_map/coarse/pallas_call | solution.py:497
Async XLA Ops:
  1.4 7.4 %collective-permute-start = (bf16[48,256]{1,0:T(8,128)(2,1)S(1)}, bf16[48,256]{1,0:T(8,128)(2,1)S(1)}, u32[]{:S(2)}, u32[]{:S(2)}) collective-permute-start(bf16[48,256]{1,0:T(8,128)(2,1)S(1)} %get-tuple-element.30), channel_id=1, source_target_pairs={{4,8},{12,16},{20,24},{8,4},{16,12},{24,20},{5,9},{13,17},{21,25},... | collective-permute-start | bytes 73736 | tf_op jit(solution)/shard_map/ppermute | solution.py:401
  2.1 6.7 %collective-permute-start.1 = (bf16[48,256]{1,0:T(8,128)(2,1)S(1)}, bf16[48,256]{1,0:T(8,128)(2,1)S(1)}, u32[]{:S(2)}, u32[]{:S(2)}) collective-permute-start(bf16[48,256]{1,0:T(8,128)(2,1)S(1)} %get-tuple-element.31), channel_id=1, source_target_pairs={{0,4},{8,12},{16,20},{24,28},{4,0},{12,8},{20,16},{28,24},{1,5},{9... | collective-permute-start | bytes 73736 | tf_op jit(solution)/shard_map/ppermute | solution.py:401
  9.0 8.3 %collective-permute-start.2 = (bf16[80,256]{1,0:T(8,128)(2,1)S(1)}, bf16[80,256]{1,0:T(8,128)(2,1)S(1)}, u32[]{:S(2)}, u32[]{:S(2)}) collective-permute-start(bf16[80,256]{1,0:T(8,128)(2,1)S(1)} %get-tuple-element.33), channel_id=1, source_target_pairs={{1,2},{2,1},{5,6},{6,5},{9,10},{10,9},{13,14},{14,13},{17,18},{18,... | collective-permute-start | bytes 122888 | tf_op jit(solution)/shard_map/ppermute | solution.py:401
  9.7 7.7 %collective-permute-start.3 = (bf16[80,256]{1,0:T(8,128)(2,1)S(1)}, bf16[80,256]{1,0:T(8,128)(2,1)S(1)}, u32[]{:S(2)}, u32[]{:S(2)}) collective-permute-start(bf16[80,256]{1,0:T(8,128)(2,1)S(1)} %get-tuple-element.34.after_ref), channel_id=1, source_target_pairs={{0,1},{2,3},{1,0},{3,2},{4,5},{6,7},{5,4},{7,6},{8,9},{10,11},{9,8... | collective-permute-start | bytes 122888 | tf_op jit(solution)/shard_map/ppermute | solution.py:401
